TPU v7x, 32 devices: a whole 2x2x4 slice. The times are simulated.
32 devices in a mesh: segment: 2 (over y), fsdp: 4 (over x, core), seq: 4 (over z).
Axes of the slice: x: 2, y: 2, z: 4, core: 2. Of those that a mesh axis runs over, the one named last changes fastest.
Arguments:
- arriving: bfloat16 [2, 4, 768, 2048], P('segment', 'fsdp', 'seq'), may hold values from -6 to 6
- gain: float32 [2, 2048], P('segment'), may hold values from 0.1 to 1.9
- input_weight: bfloat16 [2, 2048, 16, 3, 128], P('segment', 'fsdp', 'seq')
- output_weight: bfloat16 [2, 16, 128, 2048], P('segment', 'seq', None, 'fsdp'), may hold values from -1 to 1
- block_pattern: int32 [2, 4, 24, 6], P('segment', 'fsdp'), may hold values from 0 to 23, as said below
Outputs:
- passed: bfloat16 [2, 4, 768, 2048], P('segment', 'fsdp', 'seq')
Inputs may be any that keep to these rules, and one draw needn't show every extreme that they name: `block_pattern`: row j of a document lists 6 different blocks; the first three are j - 1, j and j + 1 modulo 24, and block 0 is listed in every row.
All inputs are finite; a program needn't handle non-finite values.
Results may differ from a plain program's by a relative error of at most 0.012.
Values may be sent and summed in bfloat16 or wider, within the bound.
A program may use at most 64 MiB of HBM per device.

v0:
```python
import jax
import jax.numpy as jnp
from jax import lax
from jax.sharding import PartitionSpec as P

BLOCK = 32
SEL = 6
EPSILON = 1e-05


def passed_along(value, axis, steps):
    count = lax.axis_size(axis)
    pairs = [(source, (source + steps) % count) for source in range(count)]
    return lax.ppermute(value, axis, pairs)


def normalize(tokens, gain_row):
    values = tokens.astype(jnp.float32)
    spread = jnp.mean(values * values, axis=-1, keepdims=True)
    return (values * lax.rsqrt(spread + EPSILON) * gain_row).astype(jnp.bfloat16)


def attend(projected, pattern_rows):
    length, head_group, triple, head_width = projected.shape
    block_count = length // BLOCK
    query_rows = projected[:, :, 0].reshape(block_count, BLOCK, head_group, head_width)
    key_blocks = projected[:, :, 1].reshape(block_count, BLOCK, head_group, head_width)
    value_blocks = projected[:, :, 2].reshape(block_count, BLOCK, head_group, head_width)
    key_rows = jnp.take(key_blocks, pattern_rows, axis=0).reshape(
        block_count, SEL * BLOCK, head_group, head_width
    )
    value_rows = jnp.take(value_blocks, pattern_rows, axis=0).reshape(
        block_count, SEL * BLOCK, head_group, head_width
    )
    scores = jnp.einsum(
        "qbge,qnge->gqbn", query_rows, key_rows, preferred_element_type=jnp.float32
    ) * head_width ** (-0.5)
    row_max = jnp.max(scores, axis=-1, keepdims=True)
    exponent = jnp.exp(scores - row_max)
    weights = (exponent / jnp.sum(exponent, axis=-1, keepdims=True)).astype(jnp.bfloat16)
    mixed_rows = jnp.einsum(
        "gqbn,qnge->qbge", weights, value_rows, preferred_element_type=jnp.float32
    )
    return mixed_rows.astype(jnp.bfloat16).reshape(length, head_group * head_width)


def body(arriving, gain, input_weight, output_weight, block_pattern):
    tokens = arriving[0, 0]
    row_count = tokens.shape[0]
    normed = normalize(tokens, gain[0])
    slab_rows, head_group, triple, head_size = input_weight.shape[1:]
    columns = head_group * triple * head_size
    panel_flat = input_weight[0].reshape(slab_rows, columns)
    length = row_count * lax.axis_size("seq")
    whole_panel = lax.all_gather(panel_flat, "fsdp", axis=0, tiled=True)
    projected = jnp.dot(
        lax.all_gather(normed, "seq", axis=0, tiled=True),
        whole_panel,
        preferred_element_type=jnp.float32,
    )
    projected = projected.astype(jnp.bfloat16).reshape(length, head_group, triple, head_size)
    mixed_rows = attend(projected, block_pattern[0, 0])
    out_panel = output_weight[0].reshape(head_group * head_size, -1)
    whole_out = lax.all_gather(out_panel, "fsdp", axis=1, tiled=True)
    branch = lax.psum_scatter(
        jnp.dot(mixed_rows, whole_out, preferred_element_type=jnp.float32).astype(jnp.bfloat16),
        "seq",
        scatter_dimension=0,
        tiled=True,
    ).astype(jnp.float32)
    updated = (tokens.astype(jnp.float32) + branch).astype(jnp.bfloat16)
    passed = passed_along(updated, "segment", 1)
    return passed[None, None]


def solution(mesh):
    in_specs = (
        P("segment", "fsdp", "seq", None),
        P("segment", None),
        P("segment", "fsdp", "seq", None, None),
        P("segment", "seq", None, "fsdp"),
        P("segment", "fsdp", None, None),
    )
    out_specs = P("segment", "fsdp", "seq", None)
    return jax.shard_map(body, mesh=mesh, in_specs=in_specs, out_specs=out_specs, check_vma=False)
```

profile of v0, /device:TPU:0, one launch (start us, length us, event | category | flops | bytes accessed | tf_op | source)
XLA Modules:
  0.0 277.0 jit_solution(2608817675597869169)
XLA Ops:
  6.5 1.5 fusion.4
  8.0 2.3 fusion.6
  10.3 0.0 all-gather.6.cloned.1.call-start
  10.4 2.6 copy.24
  13.0 0.0 all-gather.8.cloned.1.call-start
  13.0 0.7 all-gather.8.cloned.1.call-update
  13.7 0.0 reduce-scatter.2.cloned.1.call-start
  13.8 0.1 copy.27
  13.9 0.1 reshape.54
  14.0 0.1 copy.23
  14.1 62.6 %all-gather.4.cloned.1.call-done = bf16[768,2048]{1,0:T(8,128)(2,1)} async-done(((bf16[192,2048]{1,0:T(8,128)(2,1)}), bf16[768,2048]{1,0:T(8,128)(2,1)}) %all-gather.4.cloned.1.call-update) | async-done | bytes 3145744 | tf_op jit(solution)/shard_map/all_gather | solution.py:57
  76.7 46.6 %all-gather.6.cloned.1.call-done = bf16[2048,1536]{0,1:T(8,128)(2,1)} async-done(((bf16[512,1536]{0,1:T(8,128)(2,1)}), bf16[2048,1536]{0,1:T(8,128)(2,1)}) %all-gather.6.cloned.1.call-update) | async-done | bytes 6291472 | tf_op jit(solution)/shard_map/all_gather | solution.py:55
  123.3 9.3 %convolution_convert_fusion.1 = bf16[768,1536]{1,0:T(8,128)(2,1)} fusion(bf16[768,2048]{1,0:T(8,128)(2,1)} %all-gather.4.cloned.1.call-done, bf16[2048,1536]{0,1:T(8,128)(2,1)} %all-gather.6.cloned.1.call-done), kind=kOutput, calls=%fused_computation.6 | convolution fusion | flops 4833017856 | bytes 11796480 | tf_op jit(solution)/shard_map/dot_general | solution.py:56
  132.6 2.9 %copy.25 = bf16[768,1536]{0,1:T(8,128)(2,1)S(1)} copy(bf16[768,1536]{1,0:T(8,128)(2,1)} %convolution_convert_fusion.1) | data formatting | bytes 4718592 | tf_op jit(solution)/shard_map/convert_element_type | solution.py:61
  135.5 1.3 fusion.20
  136.8 1.5 copy.31
  138.3 1.5 copy.26
  139.8 7.6 %gather_fusion.1 = bf16[144,32,4,128]{3,1,2,0:T(8,128)(2,1)} fusion(bf16[24,32,4,128]{3,1,0,2:T(8,128)(2,1)S(1)} %bitcast.37, s32[1024]{0:T(1024)S(1)} %pad_clamp_fusion), kind=kCustom, calls=%fused_computation.1.clone | custom fusion | bytes 9437760 | tf_op jit(solution)/shard_map/jit(_take)/gather | solution.py:29
  147.4 7.6 %gather_fusion = bf16[144,32,4,128]{3,1,2,0:T(8,128)(2,1)} fusion(bf16[24,32,4,128]{3,1,0,2:T(8,128)(2,1)S(1)} %bitcast.36, s32[1024]{0:T(1024)S(1)} %pad_clamp_fusion), kind=kCustom, calls=%fused_computation.clone | custom fusion | bytes 9437760 | tf_op jit(solution)/shard_map/jit(_take)/gather | solution.py:32
  155.0 5.7 %broadcast_select_fusion = (bf16[24,6,32,4,128]{4,2,3,1,0:T(8,128)(2,1)S(1)}, bf16[24,6,32,4,128]{4,2,3,1,0:T(8,128)(2,1)}) fusion(bf16[24,6,32,4,128]{4,2,3,1,0:T(8,128)(2,1)} %bitcast.38, pred[24,6]{1,0:T(8,128)(4,1)S(1)} %copy.23, bf16[24,6,32,4,128]{4,2,3,1,0:T(8,128)(2,1)} %bitcast.39), kind=kLoop, calls=%fused_computation.3 | loop fusion | flops 4718592 | bytes 18874512 | tf_op jit(solution)/shard_map/jit(_take)/select_n | solution.py:29
  160.7 3.6 %copy.33 = bf16[24,6,32,4,128]{4,2,1,0,3:T(8,128)(2,1)} copy(bf16[24,6,32,4,128]{4,2,3,1,0:T(8,128)(2,1)S(1)} %get-tuple-element.9) | data formatting | bytes 9437184 | tf_op jit(solution)/shard_map/jit(_take)/select_n | solution.py:29
  164.2 0.4 copy.29
  164.6 5.9 %copy.28 = bf16[24,6,32,4,128]{4,2,1,3,0:T(8,128)(2,1)} copy(bf16[24,6,32,4,128]{4,2,3,1,0:T(8,128)(2,1)} %get-tuple-element.10) | data formatting | bytes 9437184 | tf_op jit(solution)/shard_map/jit(_take)/select_n | solution.py:32
  170.5 7.2 %fusion.21 = (f32[4,24,32]{2,1,0:T(8,128)S(1)}, f32[4,24,32,192]{3,2,1,0:T(8,128)}) fusion(bf16[24,32,4,128]{3,1,0,2:T(8,128)(2,1)S(1)} %bitcast.44, bf16[24,192,4,128]{3,1,0,2:T(8,128)(2,1)} %bitcast.40), kind=kOutput, calls=%fused_computation.31 | convolution fusion | flops 152764608 | bytes 7876608 | tf_op jit(solution)/shard_map/sub | solution.py:39
  177.7 5.2 %fusion.14 = bf16[24,32,4,128]{3,1,2,0:T(8,128)(2,1)S(1)} fusion(bf16[24,192,4,128]{3,1,2,0:T(8,128)(2,1)} %bitcast.43, f32[4,24,32,192]{3,2,1,0:T(8,128)} %get-tuple-element.12, f32[4,24,32]{2,1,0:T(8,128)S(1)} %get-tuple-element.11), kind=kOutput, calls=%fused_computation.22 | convolution fusion | flops 152567808 | bytes 7876608 | tf_op jit(solution)/shard_map/gqbn,qnge->qbge/dot_general | solution.py:41
  182.9 0.4 copy.35
  183.3 5.0 %convolution_convert_fusion = bf16[768,2048]{1,0:T(8,128)(2,1)} fusion(bf16[512,2048]{1,0:T(8,128)(2,1)} %all-gather.8.cloned.1.call-done, bf16[96,8,4,128]{3,2,1,0:T(4,128)(2,1)S(1)} %bitcast.45), kind=kOutput, calls=%fused_computation.5 | convolution fusion | flops 1612185600 | bytes 6029312 | tf_op jit(solution)/shard_map/dot_general | solution.py:66
  188.4 60.6 %reduce-scatter.2.cloned.1.call-done = bf16[192,2048]{1,0:T(8,128)(2,1)} async-done(((bf16[768,2048]{1,0:T(8,128)(2,1)}), bf16[192,2048]{1,0:T(8,128)(2,1)}) %reduce-scatter.2.cloned.1.call-update) | async-done | bytes 786448 | tf_op jit(solution)/shard_map/reduce_scatter | solution.py:65
  248.9 1.4 fusion.7
  250.4 1.5 collective-permute-start
  251.9 17.7 %collective-permute-done = bf16[192,2048]{1,0:T(8,128)(2,1)S(1)} collective-permute-done((bf16[192,2048]{1,0:T(8,128)(2,1)S(1)}, bf16[192,2048]{1,0:T(8,128)(2,1)S(1)}, u32[]{:S(2)}, u32[]{:S(2)}) %collective-permute-start) | collective-permute-done | bytes 786464 | tf_op jit(solution)/shard_map/ppermute | solution.py:14
  269.5 0.9 copy.52
  (15 shorter events, 0.1 us)
Async XLA Ops:
  6.5 3.8 %copy-start.1 = (bf16[1,512,4,3,128]{4,2,3,1,0:T(4,128)(2,1)S(1)}, bf16[1,512,4,3,128]{4,2,3,1,0:T(4,128)(2,1)}, u32[]{:S(2)}) copy-start(bf16[1,512,4,3,128]{4,2,3,1,0:T(4,128)(2,1)} %param.9) | copy-start | bytes 4718596
  6.5 70.1 %all-gather.4.cloned.1.call-start = ((), (), s32[]{:S(2)}) async-start(), calls=%async_computation.1 | async-start | bytes 3932160 | tf_op jit(solution)/shard_map/all_gather | solution.py:57
  10.3 3.5 %copy-start.2 = (s32[1,1,24,6]{2,1,3,0:T(1,128)S(1)}, s32[1,1,24,6]{2,1,3,0:T(1,128)}, u32[]{:S(2)}) copy-start(s32[1,1,24,6]{2,1,3,0:T(1,128)} %param.11) | copy-start | bytes 1732
  10.3 113.0 %all-gather.6.cloned.1.call-start = ((), (), s32[]{:S(2)}) async-start(), calls=%async_computation.2 | async-start | bytes 7864320 | tf_op jit(solution)/shard_map/all_gather | solution.py:55
  13.0 170.3 %all-gather.8.cloned.1.call-start = ((), (), s32[]{:S(2)}) async-start(), calls=%async_computation.3 | async-start | bytes 2621440 | tf_op jit(solution)/shard_map/all_gather | solution.py:64
  13.7 235.2 %reduce-scatter.2.cloned.1.call-start = ((), (), s32[]{:S(2)}) async-start(), calls=%async_computation.4 | async-start | bytes 3932160 | tf_op jit(solution)/shard_map/reduce_scatter | solution.py:65
  188.3 60.6 %copy-start = (bf16[1,1,192,2048]{3,2,1,0:T(8,128)(2,1)S(1)}, bf16[1,1,192,2048]{3,2,1,0:T(8,128)(2,1)}, u32[]{:S(2)}) copy-start(bf16[1,1,192,2048]{3,2,1,0:T(8,128)(2,1)} %param.7) | copy-start | bytes 2359300
  250.4 19.2 %collective-permute-start = (bf16[192,2048]{1,0:T(8,128)(2,1)S(1)}, bf16[192,2048]{1,0:T(8,128)(2,1)S(1)}, u32[]{:S(2)}, u32[]{:S(2)}) collective-permute-start(bf16[192,2048]{1,0:T(8,128)(2,1)S(1)} %fusion.7), channel_id=1, source_target_pairs={{0,16},{16,0},{1,17},{17,1},{2,18},{18,2},{3,19},{19,3},{4,20},{20... | collective-permute-start | bytes 2359304 | tf_op jit(solution)/shard_map/ppermute | solution.py:14
Sparse Core Ops, SparseCore 0:
  10.5 66.1 all-gather.3
  78.2 45.0 all-gather.5
  124.9 22.5 all-gather.7
  188.5 60.4 reduce-scatter.1
where the time goes:
time: 277 us
  waiting for transfers between devices  188 us (68%)
  local copies, waits for them, and re-layouts  36.4 us (13%)
  matrix products  26.7 us (10%)
  between operations  13.2 us (5%)
  other arithmetic  10.8 us (4%)
    all_gather x1, waiting for transfers between devices, body(): lax.all_gather(normed, 'seq', axis=0, tiled=True)  62.6 us
    reduce_scatter x1, waiting for transfers between devices, body(): lax.psum_scatter(jnp.dot(mixed_rows, whole_out, preferred_element_type=jn...  60.6 us
    all_gather x1, waiting for transfers between devices, body(): whole_panel = lax.all_gather(panel_flat, 'fsdp', axis=0, tiled=True)  46.6 us
    ppermute x1, waiting for transfers between devices, passed_along(): return lax.ppermute(value, axis, pairs)  17.7 us
    dot_general x1, matrix products, body(): jnp.dot(lax.all_gather(normed, 'seq', axis=0, tiled=True), whole_panel, p...  9.27 us
    gather x1, local copies, waits for them, and re-layouts, attend(): jnp.take(value_blocks, pattern_rows, axis=0)  7.62 us
    gather x1, local copies, waits for them, and re-layouts, attend(): jnp.take(key_blocks, pattern_rows, axis=0)  7.56 us
    sub x1, matrix products, attend(): exponent = jnp.exp(scores - row_max)  7.16 us
  transfers between devices with their start and end apart: 5, of which 4 were waited for; matrix products, arithmetic and copies ran while one was open for 23% of the time, Pallas kernels for 0%

commit v1 on v0

--- a/solution.py
+++ b/solution.py
@@ -52,7 +52,14 @@
     columns = head_group * triple * head_size
     panel_flat = input_weight[0].reshape(slab_rows, columns)
     length = row_count * lax.axis_size("seq")
-    whole_panel = lax.all_gather(panel_flat, "fsdp", axis=0, tiled=True)
+    peers = lax.axis_size("fsdp")
+    right = [(i, (i + 1) % peers) for i in range(peers)]
+    parts = [panel_flat]
+    for far in range(1, peers):
+        parts = [lax.ppermute(parts[0], "fsdp", right), *parts]
+    out = jnp.concatenate(parts, axis=0)
+    shift = (lax.axis_index("fsdp") + 1) * parts[-1].shape[0]
+    whole_panel = jnp.roll(out, shift, axis=0)
     projected = jnp.dot(
         lax.all_gather(normed, "seq", axis=0, tiled=True),
         whole_panel,

time: 277 us -> 245 us (0.88)
  waiting for transfers between devices: 188 us -> 140 us
  local copies, waits for them, and re-layouts: 36.4 us -> 51.4 us
    all_gather x1, waiting for transfers between devices: 62.6 us -> 0.01 us  [body(): lax.all_gather(normed, 'seq', axis=0, tiled=True)]
    ppermute x0 -> x3, waiting for transfers between devices: none -> 59.7 us  [body(): parts = [lax.ppermute(parts[0], 'fsdp', right), *parts]]
    all_gather x1 -> x0, waiting for transfers between devices: 46.6 us -> none  [body(): whole_panel = lax.all_gather(panel_flat, 'fsdp', axis=0, tiled=True)]
    unnamed x8 -> x15, local copies, waits for them, and re-layouts: 3.47 us -> 17.3 us
  transfers between devices with their start and end apart: 5 -> 7, of which waited for: 4 -> 5; matrix products, arithmetic and copies ran while one was open for 23% -> 32% of each run, Pallas kernels for 0% -> 0%
where the time goes in v1:
time: 245 us
  waiting for transfers between devices  140 us (57%)
  local copies, waits for them, and re-layouts  51.4 us (21%)
  matrix products  26.8 us (11%)
  between operations  13.2 us (5%)
  other arithmetic  10.9 us (4%)
    reduce_scatter x1, waiting for transfers between devices, body(): lax.psum_scatter(jnp.dot(mixed_rows, whole_out, preferred_element_type=jn...  62.7 us
    ppermute x3, waiting for transfers between devices, body(): parts = [lax.ppermute(parts[0], 'fsdp', right), *parts]  59.7 us
    ppermute x1, waiting for transfers between devices, passed_along(): return lax.ppermute(value, axis, pairs)  17.6 us
    unnamed x15, local copies, waits for them, and re-layouts  17.3 us
    dot_general x1, matrix products, body(): jnp.dot(lax.all_gather(normed, 'seq', axis=0, tiled=True), whole_panel, p...  9.33 us
    gather x1, local copies, waits for them, and re-layouts, attend(): jnp.take(key_blocks, pattern_rows, axis=0)  7.63 us
    gather x1, local copies, waits for them, and re-layouts, attend(): jnp.take(value_blocks, pattern_rows, axis=0)  7.52 us
    sub x1, matrix products, attend(): exponent = jnp.exp(scores - row_max)  7.18 us
  transfers between devices with their start and end apart: 7, of which 5 were waited for; matrix products, arithmetic and copies ran while one was open for 32% of the time, Pallas kernels for 0%

profile of v1, /device:TPU:0, one launch (start us, length us, event | category | flops | bytes accessed | tf_op | source)
XLA Modules:
  0.0 244.5 jit_solution(12368732960169958544)
XLA Ops:
  6.5 1.5 fusion.9
  8.0 2.3 fusion.11
  10.4 1.4 copy.24
  12.3 20.0 %collective-permute-done = bf16[512,1536]{0,1:T(8,128)(2,1)S(1)} collective-permute-done((bf16[512,1536]{0,1:T(8,128)(2,1)S(1)}, bf16[512,1536]{0,1:T(8,128)(2,1)S(1)}, u32[]{:S(2)}, u32[]{:S(2)}) %collective-permute-start) | collective-permute-done | bytes 1572896 | tf_op jit(solution)/shard_map/ppermute | solution.py:59
  32.4 19.9 %collective-permute-done.1 = bf16[512,1536]{0,1:T(8,128)(2,1)} collective-permute-done((bf16[512,1536]{0,1:T(8,128)(2,1)S(1)}, bf16[512,1536]{0,1:T(8,128)(2,1)}, u32[]{:S(2)}, u32[]{:S(2)}) %collective-permute-start.1) | collective-permute-done | bytes 1572896 | tf_op jit(solution)/shard_map/ppermute | solution.py:59
  52.7 19.7 %collective-permute-done.2 = bf16[512,1536]{0,1:T(8,128)(2,1)} collective-permute-done((bf16[512,1536]{0,1:T(8,128)(2,1)}, bf16[512,1536]{0,1:T(8,128)(2,1)}, u32[]{:S(2)}, u32[]{:S(2)}) %collective-permute-start.2) | collective-permute-done | bytes 1572896 | tf_op jit(solution)/shard_map/ppermute | solution.py:59
  72.5 2.8 %constant_dynamic-update-slice_fusion.7 = bf16[4096,1536]{0,1:T(8,128)(2,1)} fusion(bf16[512,1536]{0,1:T(8,128)(2,1)} %collective-permute-done.2), kind=kLoop, calls=%fused_computation.34 | loop fusion | bytes 3145728
  75.2 2.8 %constant_dynamic-update-slice_fusion.6 = bf16[4096,1536]{0,1:T(8,128)(2,1)} fusion(bf16[4096,1536]{0,1:T(8,128)(2,1)} %constant_dynamic-update-slice_fusion.7, bf16[512,1536]{0,1:T(8,128)(2,1)} %collective-permute-done.1), kind=kLoop, calls=%fused_computation.33 | loop fusion | bytes 3145728
  78.0 1.3 constant_dynamic-update-slice_fusion.5
  79.3 1.3 constant_dynamic-update-slice_fusion.4
  80.7 2.7 %constant_dynamic-update-slice_fusion.3 = bf16[4096,1536]{0,1:T(8,128)(2,1)} fusion(bf16[4096,1536]{0,1:T(8,128)(2,1)} %constant_dynamic-update-slice_fusion.4, bf16[512,1536]{0,1:T(8,128)(2,1)} %collective-permute-done.2), kind=kLoop, calls=%fused_computation.30 | loop fusion | bytes 3145728
  83.4 2.8 %constant_dynamic-update-slice_fusion.2 = bf16[4096,1536]{0,1:T(8,128)(2,1)} fusion(bf16[4096,1536]{0,1:T(8,128)(2,1)} %constant_dynamic-update-slice_fusion.3, bf16[512,1536]{0,1:T(8,128)(2,1)} %collective-permute-done.1), kind=kLoop, calls=%fused_computation.29 | loop fusion | bytes 3145728
  86.1 1.3 constant_dynamic-update-slice_fusion.1
  87.5 1.3 constant_dynamic-update-slice_fusion
  88.8 9.3 %fusion.3 = bf16[768,1536]{1,0:T(8,128)(2,1)} fusion(bf16[768,2048]{1,0:T(8,128)(2,1)} %all-gather.3.cloned.1.call-done, bf16[4096,1536]{0,1:T(8,128)(2,1)} %constant_dynamic-update-slice_fusion, s32[]{:T(128)S(6)} %select_n.21), kind=kOutput, calls=%fused_computation.7 | convolution fusion | flops 4833017856 | bytes 11796484 | tf_op jit(solution)/shard_map/dot_general | solution.py:63
  98.1 2.8 %copy.25 = bf16[768,1536]{0,1:T(8,128)(2,1)S(1)} copy(bf16[768,1536]{1,0:T(8,128)(2,1)} %fusion.3) | data formatting | bytes 4718592 | tf_op jit(solution)/shard_map/convert_element_type | solution.py:68
  100.9 1.3 fusion.26
  102.2 1.5 copy.31
  103.7 1.5 copy.26
  105.2 7.6 %gather_fusion.1 = bf16[144,32,4,128]{3,1,2,0:T(8,128)(2,1)} fusion(bf16[24,32,4,128]{3,1,0,2:T(8,128)(2,1)S(1)} %bitcast.36, s32[1024]{0:T(1024)S(1)} %pad_clamp_fusion), kind=kCustom, calls=%fused_computation.1.clone | custom fusion | bytes 9437760 | tf_op jit(solution)/shard_map/jit(_take)/gather | solution.py:29
  112.9 7.5 %gather_fusion = bf16[144,32,4,128]{3,1,2,0:T(8,128)(2,1)} fusion(bf16[24,32,4,128]{3,1,0,2:T(8,128)(2,1)S(1)} %bitcast.35, s32[1024]{0:T(1024)S(1)} %pad_clamp_fusion), kind=kCustom, calls=%fused_computation.clone | custom fusion | bytes 9437760 | tf_op jit(solution)/shard_map/jit(_take)/gather | solution.py:32
  120.4 5.7 %broadcast_select_fusion = (bf16[24,6,32,4,128]{4,2,3,1,0:T(8,128)(2,1)S(1)}, bf16[24,6,32,4,128]{4,2,3,1,0:T(8,128)(2,1)}) fusion(bf16[24,6,32,4,128]{4,2,3,1,0:T(8,128)(2,1)} %bitcast.37, pred[24,6]{1,0:T(8,128)(4,1)S(1)} %copy.23, bf16[24,6,32,4,128]{4,2,3,1,0:T(8,128)(2,1)} %bitcast.38), kind=kLoop, calls=%fused_computation.5 | loop fusion | flops 4718592 | bytes 18874512 | tf_op jit(solution)/shard_map/jit(_take)/select_n | solution.py:29
  126.1 3.5 %copy.33 = bf16[24,6,32,4,128]{4,2,1,0,3:T(8,128)(2,1)} copy(bf16[24,6,32,4,128]{4,2,3,1,0:T(8,128)(2,1)S(1)} %get-tuple-element.9) | data formatting | bytes 9437184 | tf_op jit(solution)/shard_map/jit(_take)/select_n | solution.py:29
  130.0 6.0 %copy.28 = bf16[24,6,32,4,128]{4,2,1,3,0:T(8,128)(2,1)} copy(bf16[24,6,32,4,128]{4,2,3,1,0:T(8,128)(2,1)} %get-tuple-element.10) | data formatting | bytes 9437184 | tf_op jit(solution)/shard_map/jit(_take)/select_n | solution.py:32
  135.9 7.2 %fusion.27 = (f32[4,24,32]{2,1,0:T(8,128)S(1)}, f32[4,24,32,192]{3,2,1,0:T(8,128)}) fusion(bf16[24,32,4,128]{3,1,0,2:T(8,128)(2,1)S(1)} %bitcast.45, bf16[24,192,4,128]{3,1,0,2:T(8,128)(2,1)} %bitcast.39), kind=kOutput, calls=%fused_computation.42 | convolution fusion | flops 152764608 | bytes 7876608 | tf_op jit(solution)/shard_map/sub | solution.py:39
  143.1 5.2 %fusion.19 = bf16[24,32,4,128]{3,1,2,0:T(8,128)(2,1)S(1)} fusion(bf16[24,192,4,128]{3,1,2,0:T(8,128)(2,1)} %bitcast.44, f32[4,24,32,192]{3,2,1,0:T(8,128)} %get-tuple-element.12, f32[4,24,32]{2,1,0:T(8,128)S(1)} %get-tuple-element.11), kind=kOutput, calls=%fused_computation.24 | convolution fusion | flops 152567808 | bytes 7876608 | tf_op jit(solution)/shard_map/gqbn,qnge->qbge/dot_general | solution.py:41
  148.8 5.1 %convolution_convert_fusion = bf16[768,2048]{1,0:T(8,128)(2,1)} fusion(bf16[512,2048]{1,0:T(8,128)(2,1)} %all-gather.5.cloned.1.call-done, bf16[96,8,4,128]{3,2,1,0:T(4,128)(2,1)S(1)} %bitcast.46), kind=kOutput, calls=%fused_computation.8 | convolution fusion | flops 1612185600 | bytes 6029312 | tf_op jit(solution)/shard_map/dot_general | solution.py:73
  153.9 62.7 %reduce-scatter.2.cloned.1.call-done = bf16[192,2048]{1,0:T(8,128)(2,1)} async-done(((bf16[768,2048]{1,0:T(8,128)(2,1)}), bf16[192,2048]{1,0:T(8,128)(2,1)}) %reduce-scatter.2.cloned.1.call-update) | async-done | bytes 786448 | tf_op jit(solution)/shard_map/reduce_scatter | solution.py:72
  216.6 1.4 fusion.12
  218.0 1.5 collective-permute-start.3
  219.5 17.6 %collective-permute-done.3 = bf16[192,2048]{1,0:T(8,128)(2,1)S(1)} collective-permute-done((bf16[192,2048]{1,0:T(8,128)(2,1)S(1)}, bf16[192,2048]{1,0:T(8,128)(2,1)S(1)}, u32[]{:S(2)}, u32[]{:S(2)}) %collective-permute-start.3) | collective-permute-done | bytes 786464 | tf_op jit(solution)/shard_map/ppermute | solution.py:14
  237.1 0.9 copy.59
  (26 shorter events, 1.8 us)
Async XLA Ops:
  6.5 3.8 %copy-start.1 = (bf16[1,512,4,3,128]{4,2,3,1,0:T(4,128)(2,1)S(1)}, bf16[1,512,4,3,128]{4,2,3,1,0:T(4,128)(2,1)}, u32[]{:S(2)}) copy-start(bf16[1,512,4,3,128]{4,2,3,1,0:T(4,128)(2,1)} %param.9) | copy-start | bytes 4718596
  6.5 82.2 %all-gather.3.cloned.1.call-start = ((), (), s32[]{:S(2)}) async-start(), calls=%async_computation.1 | async-start | bytes 3932160 | tf_op jit(solution)/shard_map/all_gather | solution.py:64
  8.0 44.4 %copy-start.2 = (s32[1,1,24,6]{2,1,3,0:T(1,128)S(1)}, s32[1,1,24,6]{2,1,3,0:T(1,128)}, u32[]{:S(2)}) copy-start(s32[1,1,24,6]{2,1,3,0:T(1,128)} %param.11) | copy-start | bytes 1732
  10.3 138.4 %all-gather.5.cloned.1.call-start = ((), (), s32[]{:S(2)}) async-start(), calls=%async_computation.2 | async-start | bytes 2621440 | tf_op jit(solution)/shard_map/all_gather | solution.py:71
  11.8 20.5 %collective-permute-start = (bf16[512,1536]{0,1:T(8,128)(2,1)S(1)}, bf16[512,1536]{0,1:T(8,128)(2,1)S(1)}, u32[]{:S(2)}, u32[]{:S(2)}) collective-permute-start(bf16[512,1536]{0,1:T(8,128)(2,1)S(1)} %bitcast.40), channel_id=1, source_target_pairs={{0,4},{4,8},{8,12},{12,0},{1,5},{5,9},{9,13},{13,1},{2,6},{6,10},{... | collective-permute-start | bytes 4718600 | tf_op jit(solution)/shard_map/ppermute | solution.py:59
  32.4 19.9 %collective-permute-start.1 = (bf16[512,1536]{0,1:T(8,128)(2,1)S(1)}, bf16[512,1536]{0,1:T(8,128)(2,1)}, u32[]{:S(2)}, u32[]{:S(2)}) collective-permute-start(bf16[512,1536]{0,1:T(8,128)(2,1)S(1)} %collective-permute-done), channel_id=1, source_target_pairs={{0,4},{4,8},{8,12},{12,0},{1,5},{5,9},{9,13},{13,1},{2,6},{6,10},{... | collective-permute-start | bytes 4718600 | tf_op jit(solution)/shard_map/ppermute | solution.py:59
  52.3 20.2 %collective-permute-start.2 = (bf16[512,1536]{0,1:T(8,128)(2,1)}, bf16[512,1536]{0,1:T(8,128)(2,1)}, u32[]{:S(2)}, u32[]{:S(2)}) collective-permute-start(bf16[512,1536]{0,1:T(8,128)(2,1)} %collective-permute-done.1), channel_id=1, source_target_pairs={{0,4},{4,8},{8,12},{12,0},{1,5},{5,9},{9,13},{13,1},{2,6},{6,10},{... | collective-permute-start | bytes 4718600 | tf_op jit(solution)/shard_map/ppermute | solution.py:59
  52.3 164.2 %reduce-scatter.2.cloned.1.call-start = ((), (), s32[]{:S(2)}) async-start(), calls=%async_computation.3 | async-start | bytes 3932160 | tf_op jit(solution)/shard_map/reduce_scatter | solution.py:72
  153.8 62.7 %copy-start = (bf16[1,1,192,2048]{3,2,1,0:T(8,128)(2,1)S(1)}, bf16[1,1,192,2048]{3,2,1,0:T(8,128)(2,1)}, u32[]{:S(2)}) copy-start(bf16[1,1,192,2048]{3,2,1,0:T(8,128)(2,1)} %param.7) | copy-start | bytes 2359300
  218.0 19.2 %collective-permute-start.3 = (bf16[192,2048]{1,0:T(8,128)(2,1)S(1)}, bf16[192,2048]{1,0:T(8,128)(2,1)S(1)}, u32[]{:S(2)}, u32[]{:S(2)}) collective-permute-start(bf16[192,2048]{1,0:T(8,128)(2,1)S(1)} %fusion.12), channel_id=1, source_target_pairs={{0,16},{16,0},{1,17},{17,1},{2,18},{18,2},{3,19},{19,3},{4,20},{20... | collective-permute-start | bytes 2359304 | tf_op jit(solution)/shard_map/ppermute | solution.py:14
Sparse Core Ops, SparseCore 0:
  10.5 66.1 all-gather.2
  78.2 21.2 all-gather.4
  154.0 62.5 reduce-scatter.1
